TPU v7x, 32 devices: a whole 2x2x4 slice. The times are simulated.
32 devices in a mesh: grp: 4 (over x, core), usr: 8 (over z, y).
Axes of the slice: x: 2, y: 2, z: 4, core: 2. Of those that a mesh axis runs over, the one named last changes fastest.
Arguments:
- candidates: bfloat16 [8192, 1024], P(('grp', 'usr')), may hold values from -6 to 6
- hist_kv: bfloat16 [32, 384, 2048], P(('grp', 'usr')), may hold values from -6 to 6
- hist_len: int32 [32], P(('grp', 'usr')), may hold values from 1 to 384, as said below
- block_mask: int32 [32, 3], P(('grp', 'usr')), may hold values 0 or 1
- tile_user: int32 [128, 1], P(('grp', 'usr')), may hold values from 0 to 7; in each aligned block of 4 rows (0 to 3, 4 to 7, ...) no two rows name the same one
- tile_count: int32 [128], P(('grp', 'usr')), may hold values from 1 to 64, as said below
- weight_in: bfloat16 [1024, 4096], P(None, ('grp', 'usr')), may hold values from -0.1875 to 0.1875
- weight_out: bfloat16 [1024, 1024], P(('grp', 'usr')), may hold values from -0.1875 to 0.1875
Outputs:
- scored: bfloat16 [8192, 1024], P(('grp', 'usr'))
Inputs may be any that keep to these rules, and one draw needn't show every extreme that they name: `hist_len`: some user's history has exactly 384 items. `tile_count`: the first tile of every device is full. A tile's live candidates take its first slots. `tile_user`: the tiles of one device belong to distinct users of its group.
All inputs are finite; a program needn't handle non-finite values. No bound on the sum of `block_mask` on one device may be relied on, other than what follows from the above.
Results may differ from a plain program's by a relative error of at most 0.0057.
Values may be sent and summed in bfloat16 or wider, within the bound.
A program may use at most 128 MiB of HBM per device.

v0:
```python
import math

import jax
import jax.numpy as jnp
from jax import lax
from jax.sharding import PartitionSpec as P

HEADS = 8
BLK = 128


def norm_rows(values_in):
    centred = values_in - jnp.mean(values_in, axis=-1, keepdims=True)
    variance = jnp.mean(centred * centred, axis=-1, keepdims=True)
    return centred * lax.rsqrt(variance + 1e-05)


def attend_rows(query_rows, hist_keys, hist_values, live_items, score_scale):
    row_total = query_rows.shape[0]
    model_width = query_rows.shape[1]
    head_dim = model_width // HEADS
    query_heads = query_rows.reshape(row_total, HEADS, head_dim)
    key_heads = hist_keys.reshape(-1, HEADS, head_dim)
    value_heads = hist_values.reshape(-1, HEADS, head_dim)
    scores = (
        jnp.einsum("nhd,lhd->hnl", query_heads, key_heads, preferred_element_type=jnp.float32)
        * score_scale
    )
    weights = (jax.nn.silu(scores) * live_items).astype(jnp.bfloat16)
    attended = jnp.einsum("hnl,lhd->nhd", weights, value_heads, preferred_element_type=jnp.float32)
    return attended.reshape(row_total, model_width)


def own_term(queries, self_keys, self_values, score_scale):
    row_total = queries.shape[0]
    products = (queries.astype(jnp.float32) * self_keys.astype(jnp.float32)).reshape(
        row_total, HEADS, -1
    )
    strength = jax.nn.silu(jnp.sum(products, axis=2) * score_scale)
    value_heads = self_values.astype(jnp.float32).reshape(row_total, HEADS, -1)
    return (strength[:, :, None] * value_heads).reshape(row_total, -1)


def holder_attend(incoming, hist_keys, hist_values, live_items, score_scale):
    slot_total, item_count, model_width = incoming.shape
    per_group = math.gcd(slot_total, max(1, 512 // item_count))
    group_total = slot_total // per_group

    def answer_rows(row_block):
        return attend_rows(row_block, hist_keys, hist_values, live_items, score_scale).astype(
            jnp.bfloat16
        )

    row_blocks = incoming.reshape(group_total, per_group * item_count, model_width)
    answered = lax.map(answer_rows, row_blocks)
    return answered.reshape(slot_total, item_count, model_width)


def shards(candidates, hist_kv, hist_len, block_mask, tile_user, tile_count, weight_in, weight_out):
    row_total, model_width = candidates.shape
    tiles_here = tile_user.shape[0]
    tile_rows = row_total // tiles_here
    score_scale = (model_width // HEADS) ** (-0.5)
    holders = lax.axis_size("usr")
    normed = norm_rows(candidates.astype(jnp.float32)).astype(jnp.bfloat16)
    projected = jax.nn.silu(
        jnp.dot(
            normed,
            lax.all_gather(weight_in, ("grp", "usr"), axis=1, tiled=True),
            preferred_element_type=jnp.float32,
        )
    ).astype(jnp.bfloat16)
    queries = projected[:, :model_width]
    self_keys = projected[:, model_width : 2 * model_width]
    self_values = projected[:, 2 * model_width : 3 * model_width]
    gate_units = projected[:, 3 * model_width :]
    own_part = own_term(queries, self_keys, self_values, score_scale)
    tile_dest = tile_user[:, 0]
    outgoing = jnp.zeros((holders, tile_rows, model_width), jnp.bfloat16)
    outgoing = outgoing.at[tile_dest].set(queries.reshape(tiles_here, tile_rows, model_width))
    hist_keys = hist_kv[0, :, :model_width]
    hist_values = hist_kv[0, :, model_width:]
    positions = jnp.arange(hist_kv.shape[1], dtype=jnp.int32)
    live_items = ((positions < hist_len[0]) & (jnp.repeat(block_mask[0], BLK) > 0)).astype(
        jnp.float32
    )
    incoming = lax.all_to_all(outgoing, "usr", split_axis=0, concat_axis=0, tiled=True)
    returned = lax.all_to_all(
        holder_attend(incoming, hist_keys, hist_values, live_items, score_scale),
        "usr",
        split_axis=0,
        concat_axis=0,
        tiled=True,
    )
    history = returned[tile_dest].reshape(row_total, model_width)
    combined = history.astype(jnp.float32) + own_part
    gated_rows = (norm_rows(combined) * gate_units.astype(jnp.float32)).astype(jnp.bfloat16)
    mixed_rows = jnp.dot(
        gated_rows,
        lax.all_gather(weight_out, ("grp", "usr"), axis=0, tiled=True),
        preferred_element_type=jnp.float32,
    )
    mixed_rows = mixed_rows + candidates.astype(jnp.float32)
    live_rows = (jnp.arange(tile_rows, dtype=jnp.int32)[None, :] < tile_count[:, None]).reshape(-1)
    return jnp.where(live_rows[:, None], mixed_rows, 0.0).astype(jnp.bfloat16)


def solution(mesh):
    in_specs = (
        P(("grp", "usr"), None),
        P(("grp", "usr"), None, None),
        P(("grp", "usr")),
        P(("grp", "usr"), None),
        P(("grp", "usr"), None),
        P(("grp", "usr")),
        P(None, ("grp", "usr")),
        P(("grp", "usr"), None),
    )
    out_specs = P(("grp", "usr"), None)
    return jax.shard_map(shards, mesh=mesh, in_specs=in_specs, out_specs=out_specs, check_vma=False)
```

profile of v0, /device:TPU:1, one launch (start us, length us, event | category | flops | bytes accessed | tf_op | source)
XLA Modules:
  0.0 204.3 jit_solution(8986118018180690720)
XLA Ops:
  6.5 0.7 all-gather.3.cloned.1.call-update
  7.3 1.2 convert_reduce_fusion
  8.5 1.3 fusion.9
  9.8 0.7 fusion.25
  10.4 94.6 %all-gather.3.cloned.1.call-done = bf16[1024,4096]{1,0:T(8,128)(2,1)} async-done(((bf16[1024,128]{1,0:T(8,128)(2,1)}), bf16[1024,4096]{1,0:T(8,128)(2,1)}) %all-gather.3.cloned.1.call-update) | async-done | bytes 8388624 | tf_op jit(solution)/shard_map/all_gather | solution.py:69
  105.1 6.1 %multiply_convert_fusion.1 = bf16[256,4096]{1,0:T(8,128)(2,1)S(1)} fusion(bf16[1024,4096]{1,0:T(8,128)(2,1)} %all-gather.3.cloned.1.call-done, bf16[256,1024]{1,0:T(8,128)(2,1)} %param.8, f32[256]{0:T(256)S(1)} %add_rsqrt_fusion.1, f32[256]{0:T(256)S(1)} %broadcast_multiply_fusion.1), kind=kOutput, calls=%fused_computation.3 | convolution fusion | flops 2153775104 | bytes 11012096 | tf_op jit(solution)/shard_map/dot_general | solution.py:67
  111.2 1.3 copy-done
  112.6 1.1 broadcast_in_dim.18
  113.7 2.5 %scatter_fusion = bf16[8,64,1024]{2,1,0:T(8,128)(2,1)} fusion(bf16[8,64,1024]{2,1,0:T(8,128)(2,1)} %broadcast_in_dim.18, s32[4]{0:T(128)S(1)} %fusion.25, bf16[4,64,1024]{2,1,0:T(8,128)(2,1)S(1)} %bitcast.36), kind=kCustom, calls=%fused_computation.1 | custom fusion | bytes 1572880 | tf_op jit(solution)/shard_map/scatter | solution.py:80
  116.2 3.6 %all-to-all-start = ((bf16[8,64,1024]{2,1,0:T(8,128)(2,1)}), bf16[8,64,1024]{2,1,0:T(8,128)(2,1)S(1)}, u32[]{:S(2)}, u32[]{:S(2)}) async-start(bf16[8,64,1024]{2,1,0:T(8,128)(2,1)} %scatter_fusion), calls=%async_computation | async-start | bytes 2097152 | tf_op jit(solution)/shard_map/all_to_all | solution.py:87
  119.8 0.7 all-gather.5.cloned.1.call-update
  120.5 1.5 fusion.30
  122.0 0.4 copy.32
  122.4 1.2 copy.33
  124.3 22.0 %all-to-all-done = bf16[8,64,1024]{2,1,0:T(8,128)(2,1)S(1)} async-done(((bf16[8,64,1024]{2,1,0:T(8,128)(2,1)}), bf16[8,64,1024]{2,1,0:T(8,128)(2,1)S(1)}, u32[]{:S(2)}, u32[]{:S(2)}) %all-to-all-start) | async-done | bytes 1048608 | tf_op jit(solution)/shard_map/all_to_all | solution.py:87
  146.3 0.3 copy.34
  146.5 4.9 %fusion.4 = bf16[512,8,128]{2,0,1:T(8,128)(2,1)} fusion(bf16[384,8,128]{0,2,1:T(8,128)(2,1)} %bitcast.39, f32[384]{0:T(512)S(1)} %fusion.24, bf16[384,8,128]{0,2,1:T(8,128)(2,1)S(1)} %bitcast.38, bf16[512,8,128]{2,1,0:T(8,128)(2,1)S(1)} %bitcast.37), kind=kOutput, calls=%fused_computation.10 | convolution fusion | flops 816840704 | bytes 3671552 | tf_op jit(solution)/shard_map/while/body/eval_jaxpr/hnl,lhd->nhd/dot_general | solution.py:30
  151.4 2.1 %copy.27 = bf16[512,8,128]{2,1,0:T(8,128)(2,1)S(1)} copy(bf16[512,8,128]{2,0,1:T(8,128)(2,1)} %fusion.4) | data formatting | bytes 2097152 | tf_op jit(solution)/shard_map/while/body/eval_jaxpr/convert_element_type | solution.py:50
  153.5 1.3 convert_element_type.63
  154.8 4.1 %all-to-all-start.1 = ((bf16[8,64,1024]{2,1,0:T(8,128)(2,1)}), bf16[8,64,1024]{2,1,0:T(8,128)(2,1)S(1)}, u32[]{:S(2)}, u32[]{:S(2)}) async-start(bf16[8,64,1024]{2,1,0:T(8,128)(2,1)} %convert_element_type.63), calls=%async_computation.1 | async-start | bytes 2097152 | tf_op jit(solution)/shard_map/all_to_all | solution.py:88
  158.9 0.1 lt.39
  159.0 0.2 multiply_bitcast_fusion
  159.2 0.2 copy.35
  159.4 0.3 reduce_sum.47
  159.9 0.1 copy.29
  160.0 30.6 %all-to-all-done.1 = bf16[8,64,1024]{2,1,0:T(8,128)(2,1)S(1)} async-done(((bf16[8,64,1024]{2,1,0:T(8,128)(2,1)}), bf16[8,64,1024]{2,1,0:T(8,128)(2,1)S(1)}, u32[]{:S(2)}, u32[]{:S(2)}) %all-to-all-start.1) | async-done | bytes 1048608 | tf_op jit(solution)/shard_map/all_to_all | solution.py:88
  190.6 0.6 gather_fusion
  191.2 0.3 mul.94
  191.5 1.3 fusion.28
  192.9 0.2 multiply_reduce_fusion
  193.2 1.0 all-gather.5.cloned.1.call-done
  194.1 3.3 %fusion.6 = bf16[256,1024]{1,0:T(8,128)(2,1)} fusion(bf16[256,1024]{1,0:T(8,128)(2,1)S(1)} %copy-done.2, bf16[1024,1024]{1,0:T(8,128)(2,1)} %all-gather.5.cloned.1.call-done, f32[256,1024]{1,0:T(8,128)S(1)} %get-tuple-element.16, bf16[256,4096]{1,0:T(8,128)(2,1)} %copy-done, f32[256]{0:T(256)S(1)} %add_rsqrt_fusion, f32[256]{0:T(256)S(1)} %broadcast_multiply_fusion, ...), kind=kOutput, calls=%fused_computation.12 | convolution fusion | flops 539230208 | bytes 4720896 | tf_op jit(solution)/shard_map/dot_general | solution.py:98
  (22 shorter events, 0.4 us)
Async XLA Ops:
  6.5 98.5 %all-gather.3.cloned.1.call-start = ((), (), s32[]{:S(2)}) async-start(), calls=%async_computation.2 | async-start | bytes 8650752 | tf_op jit(solution)/shard_map/all_gather | solution.py:69
  111.2 1.3 copy-start
  112.6 9.4 %copy-start.3 = (s32[1,3]{1,0:T(1,128)S(1)}, s32[1,3]{1,0:T(1,128)}, u32[]{:S(2)}) copy-start(s32[1,3]{1,0:T(1,128)} %param.11) | copy-start | bytes 40
  116.2 30.1 %all-to-all-start = ((bf16[8,64,1024]{2,1,0:T(8,128)(2,1)}), bf16[8,64,1024]{2,1,0:T(8,128)(2,1)S(1)}, u32[]{:S(2)}, u32[]{:S(2)}) async-start(bf16[8,64,1024]{2,1,0:T(8,128)(2,1)} %scatter_fusion), calls=%async_computation | async-start | bytes 2097152 | tf_op jit(solution)/shard_map/all_to_all | solution.py:87
  119.7 74.4 %all-gather.5.cloned.1.call-start = ((), (), s32[]{:S(2)}) async-start(), calls=%async_computation.3 | async-start | bytes 2162688 | tf_op jit(solution)/shard_map/all_gather | solution.py:100
  151.4 7.4 %copy-start.4 = (s32[4]{0:T(128)S(1)}, s32[4]{0:T(128)}, u32[]{:S(2)}) copy-start(s32[4]{0:T(128)} %param.13) | copy-start | bytes 52
  151.4 7.6 %copy-start.1 = (bf16[256,4096]{1,0:T(8,128)(2,1)S(1)}, bf16[256,4096]{1,0:T(8,128)(2,1)}, u32[]{:S(2)}) copy-start(bf16[256,4096]{1,0:T(8,128)(2,1)} %copy-done) | copy-start | bytes 6291460
  154.8 35.8 %all-to-all-start.1 = ((bf16[8,64,1024]{2,1,0:T(8,128)(2,1)}), bf16[8,64,1024]{2,1,0:T(8,128)(2,1)S(1)}, u32[]{:S(2)}, u32[]{:S(2)}) async-start(bf16[8,64,1024]{2,1,0:T(8,128)(2,1)} %convert_element_type.63), calls=%async_computation.1 | async-start | bytes 2097152 | tf_op jit(solution)/shard_map/all_to_all | solution.py:88
  159.4 34.7 %copy-start.2 = (bf16[256,1024]{1,0:T(8,128)(2,1)S(1)}, bf16[256,1024]{1,0:T(8,128)(2,1)}, u32[]{:S(2)}) copy-start(bf16[256,1024]{1,0:T(8,128)(2,1)} %param.8) | copy-start | bytes 1572868
Sparse Core Ops, SparseCore 0:
  10.2 94.7 all-gather.2
  123.6 70.5 all-gather.4
where the time goes:
time: 206 us; the launch traced here: 204 us
  waiting for transfers between devices  150 us (73%)
  matrix products  14.4 us (7%)
  between operations  14.2 us (7%)
  local copies, waits for them, and re-layouts  13 us (6%)
  starting transfers between devices  7.66 us (4%)
  other arithmetic  5.47 us (3%)
    all_gather x1, waiting for transfers between devices, shards(): lax.all_gather(weight_in, ('grp', 'usr'), axis=1, tiled=True)  94.6 us
    all_to_all x1, waiting for transfers between devices, shards(): lax.all_to_all(holder_attend(incoming, hist_keys, hist_values, live_items...  30.6 us
    all_to_all x1, waiting for transfers between devices, shards(): lax.all_to_all(outgoing, 'usr', split_axis=0, concat_axis=0, tiled=True)  22 us
    dot_general x1, matrix products, shards(): jnp.dot(normed, lax.all_gather(weight_in, ('grp', 'usr'), axis=1, tiled=T...  6.12 us
    dot_general x1, matrix products, attend_rows(): jnp.einsum('hnl,lhd->nhd', weights, value_heads, preferred_element_type=j...  4.9 us
  transfers between devices with their start and end apart: 4, of which 4 were waited for; matrix products, arithmetic and copies ran while one was open for 9% of the time, Pallas kernels for 0%

commit v1 on v0

--- a/solution.py
+++ b/solution.py
@@ -1,12 +1,16 @@
+import functools
 import math
 
 import jax
 import jax.numpy as jnp
 from jax import lax
+from jax.experimental import pallas as pl
+from jax.experimental.pallas import tpu as pltpu
 from jax.sharding import PartitionSpec as P
 
 HEADS = 8
 BLK = 128
+MESH = pl.DeviceIdType.MESH
 
 
 def norm_rows(values_in):
@@ -105,6 +109,363 @@
     return jnp.where(live_rows[:, None], mixed_rows, 0.0).astype(jnp.bfloat16)
 
 
+def silu(v):
+    return v / (1.0 + jnp.exp(-v))
+
+
+def layer_kernel(
+    n_usr,
+    cand_ref,
+    kv_ref,
+    len_ref,
+    mask_ref,
+    user_ref,
+    count_ref,
+    win_ref,
+    wout_ref,
+    out_ref,
+    normed,
+    w_all,
+    wo_all,
+    proj,
+    own,
+    outgoing,
+    incoming,
+    answers,
+    returned,
+    gated,
+    w_recv,
+    o_recv,
+    w_send,
+    o_send,
+    q_recv,
+    q_send,
+    a_recv,
+    a_send,
+):
+    depth, width = win_ref.shape
+    out_rows = wout_ref.shape[0]
+    row_total, model_width = cand_ref.shape
+    tiles = user_ref.shape[0]
+    tile_rows = row_total // tiles
+    items = kv_ref.shape[1]
+    scale = width ** (-0.5)
+    g, u = lax.axis_index("grp"), lax.axis_index("usr")
+    n_z = n_usr // 2
+    x, c = g // 2, g % 2
+    z, y = u // 2, u % 2
+    to_x = ((1 - x) * 2 + c, u)
+    to_c = (x * 2 + (1 - c), u)
+    to_y = (g, z * 2 + (1 - y))
+
+    def slot_of(xx, cc, yy, zz):
+        return (xx * 2 + cc) * n_usr + zz * 2 + yy
+
+    def w_copy(slot, part, target, sem):
+        half = depth // 2
+        lo, size = (0, depth) if part is None else (part * half, half)
+        view = w_all.at[slot, pl.ds(lo, size), :]
+        return pltpu.make_async_remote_copy(
+            src_ref=view,
+            dst_ref=view,
+            send_sem=w_send.at[sem],
+            recv_sem=w_recv.at[slot, part or 0],
+            device_id=target,
+            device_id_type=MESH,
+        )
+
+    def o_copy(slot, part, target, sem):
+        half = out_rows // 2
+        lo, size = (0, out_rows) if part is None else (part * half, half)
+        view = wo_all.at[slot, pl.ds(lo, size), :]
+        return pltpu.make_async_remote_copy(
+            src_ref=view,
+            dst_ref=view,
+            send_sem=o_send.at[sem],
+            recv_sem=o_recv.at[slot, part or 0],
+            device_id=target,
+            device_id_type=MESH,
+        )
+
+    def sends_own():
+        me = slot_of(x, c, y, z)
+        listed = [(me, None, (g, ((z + k) % n_z) * 2 + y), k - 1) for k in range(1, n_z)]
+        return listed + [(me, None, to_x, 3), (me, None, to_y, 4), (me, None, to_c, 5)]
+
+    def sends_line(k):
+        slot = slot_of(x, c, y, (z + k) % n_z)
+        base = 6 + (k - 1) * 3
+        return [(slot, None, to_x, base), (slot, None, to_y, base + 1), (slot, None, to_c, base + 2)]
+
+    def sends_y(k):
+        slot = slot_of(x, c, 1 - y, (z + k) % n_z)
+        base = 15 + k * 2
+        return [(slot, 0, to_x, base), (slot, None, to_c, base + 1)]
+
+    def sends_x(k):
+        slot = slot_of(1 - x, c, y, (z + k) % n_z)
+        base = 23 + k * 2
+        return [(slot, 1, to_y, base), (slot, None, to_c, base + 1)]
+
+    def sends_corner(k, part):
+        slot = slot_of(1 - x, c, 1 - y, (z + k) % n_z)
+        return [(slot, part, to_c, 31 + k * 2 + part)]
+
+    def start_all(copy, listed):
+        for entry in listed:
+            copy(*entry).start()
+
+    def arrived(copy, slot, part):
+        copy(slot, part, to_c, 0).wait_recv()
+
+    def relay(slot, part, listed):
+        arrived(w_copy, slot, part)
+        start_all(w_copy, listed)
+        arrived(o_copy, slot, part)
+        start_all(o_copy, listed)
+
+    def project(slot):
+        block = silu(jnp.dot(normed[...], w_all[slot], preferred_element_type=jnp.float32))
+        proj[slot] = block.astype(jnp.bfloat16).reshape(tiles, tile_rows, width)
+
+    barrier = pltpu.get_barrier_semaphore()
+    peers = [to_x, to_c] + [(g, (u + k) % n_usr) for k in range(1, n_usr)]
+    for peer in peers:
+        pl.semaphore_signal(barrier, inc=1, device_id=peer, device_id_type=MESH)
+    mine = slot_of(x, c, y, z)
+    w_all[mine] = win_ref[...]
+    wo_all[mine] = wout_ref[...]
+    pl.semaphore_wait(barrier, len(peers))
+
+    start_all(w_copy, sends_own())
+    start_all(o_copy, sends_own())
+    normed[...] = norm_rows(cand_ref[...].astype(jnp.float32)).astype(jnp.bfloat16)
+    project(mine)
+
+    def line_step(k, carry):
+        slot = slot_of(x, c, y, (z + k) % n_z)
+        relay(slot, None, sends_line(k))
+        project(slot)
+        return carry
+
+    lax.fori_loop(1, n_z, line_step, 0)
+
+    def take(slot, parts):
+        for part in parts:
+            arrived(w_copy, slot, part)
+            arrived(o_copy, slot, part)
+        project(slot)
+
+    def side_step(k, carry):
+        zz = (z + k) % n_z
+        slot_y, slot_x = slot_of(x, c, 1 - y, zz), slot_of(1 - x, c, y, zz)
+        relay(slot_y, None, sends_y(k))
+        relay(slot_x, None, sends_x(k))
+        project(slot_y)
+        project(slot_x)
+        take(slot_of(x, 1 - c, y, zz), (None,))
+        return carry
+
+    lax.fori_loop(0, n_z, side_step, 0)
+
+    def corner_step(k, carry):
+        zz = (z + k) % n_z
+        slot = slot_of(1 - x, c, 1 - y, zz)
+        for part in range(2):
+            relay(slot, part, sends_corner(k, part))
+        project(slot)
+        take(slot_of(x, 1 - c, 1 - y, zz), (None,))
+        take(slot_of(1 - x, 1 - c, y, zz), (None,))
+        return carry
+
+    lax.fori_loop(0, n_z, corner_step, 0)
+
+    def last_step(k, carry):
+        take(slot_of(1 - x, 1 - c, 1 - y, (z + k) % n_z), (0, 1))
+        return carry
+
+    lax.fori_loop(0, n_z, last_step, 0)
+
+    def query_copy(k):
+        holder = (u + k) % n_usr
+        return pltpu.make_async_remote_copy(
+            src_ref=outgoing.at[holder],
+            dst_ref=incoming.at[u],
+            send_sem=q_send.at[k],
+            recv_sem=q_recv.at[k],
+            device_id=(g, holder),
+            device_id_type=MESH,
+        )
+
+    def answer_copy(k):
+        source = (u + n_usr - k) % n_usr
+        return pltpu.make_async_remote_copy(
+            src_ref=answers.at[source],
+            dst_ref=returned.at[u],
+            send_sem=a_send.at[k],
+            recv_sem=a_recv.at[k],
+            device_id=(g, source),
+            device_id_type=MESH,
+        )
+
+    def tile_for(holder):
+        chosen = 0
+        for t in range(tiles):
+            chosen = jnp.where(user_ref[t, 0] == holder, t, chosen)
+        return chosen
+
+    def dispatch_step(k, carry):
+        holder = (u + k) % n_usr
+        tile = tile_for(holder)
+        for h in range(HEADS):
+            outgoing[holder, h] = proj[h, tile]
+        query_copy(k).start()
+        return carry
+
+    lax.fori_loop(1, n_usr, dispatch_step, 0)
+    own_tile = tile_for(u)
+    for h in range(HEADS):
+        incoming[u, h] = proj[h, own_tile]
+
+    positions = lax.broadcasted_iota(jnp.int32, (1, items), 1)
+    kept = jnp.zeros((1, items), jnp.int32)
+    for b in range(items // BLK):
+        kept = jnp.where(positions // BLK == b, mask_ref[0, b], kept)
+    live = jnp.where((positions < len_ref[0]) & (kept > 0), 1.0, 0.0)
+
+    def attend(slot, dest):
+        for h in range(HEADS):
+            keys = kv_ref[0, :, h * width : (h + 1) * width]
+            values = kv_ref[0, :, model_width + h * width : model_width + (h + 1) * width]
+            scores = lax.dot_general(
+                incoming[slot, h], keys, (((1,), (1,)), ((), ())), preferred_element_type=jnp.float32
+            )
+            weights = (silu(scores * scale) * live).astype(jnp.bfloat16)
+            dest[slot, h] = jnp.dot(weights, values, preferred_element_type=jnp.float32).astype(
+                jnp.bfloat16
+            )
+
+    attend(u, returned)
+
+    def own_step(h, carry):
+        queries = proj[h].astype(jnp.float32)
+        keys = proj[HEADS + h].astype(jnp.float32)
+        strength = silu(jnp.sum(queries * keys, axis=-1, keepdims=True) * scale)
+        own[h] = strength * proj[2 * HEADS + h].astype(jnp.float32)
+        return carry
+
+    lax.fori_loop(0, HEADS, own_step, 0)
+
+    def answer_step(k, carry):
+        query_copy(k).wait_recv()
+        attend((u + n_usr - k) % n_usr, answers)
+        answer_copy(k).start()
+        return carry
+
+    lax.fori_loop(1, n_usr, answer_step, 0)
+
+    def return_step(k, carry):
+        answer_copy(k).wait_recv()
+        return carry
+
+    lax.fori_loop(1, n_usr, return_step, 0)
+
+    def tile_step(t, carry):
+        holder = user_ref[t, 0]
+        combined = jnp.concatenate(
+            [returned[holder, h].astype(jnp.float32) + own[h, t] for h in range(HEADS)], axis=-1
+        )
+        units = jnp.concatenate([proj[3 * HEADS + h, t] for h in range(HEADS)], axis=-1)
+        gated[t] = (norm_rows(combined) * units.astype(jnp.float32)).astype(jnp.bfloat16)
+        return carry
+
+    lax.fori_loop(0, tiles, tile_step, 0)
+
+    slots_here = lax.broadcasted_iota(jnp.int32, (tile_rows, 1), 0)
+    for lo in range(0, model_width, 256):
+        weights = wo_all[:, :, lo : lo + 256].reshape(model_width, 256)
+        mixed = jnp.dot(
+            gated[...].reshape(row_total, model_width), weights, preferred_element_type=jnp.float32
+        )
+        for t in range(tiles):
+            rows = slice(t * tile_rows, (t + 1) * tile_rows)
+            total = mixed[rows] + cand_ref[rows, lo : lo + 256].astype(jnp.float32)
+            out_ref[rows, lo : lo + 256] = jnp.where(slots_here < count_ref[t], total, 0.0).astype(
+                jnp.bfloat16
+            )
+
+    def sent_all(listed):
+        for entry in listed:
+            w_copy(*entry).wait_send()
+            o_copy(*entry).wait_send()
+
+    def sent_line(k, carry):
+        sent_all(sends_line(k))
+        return carry
+
+    def sent_rest(k, carry):
+        sent_all(sends_y(k) + sends_x(k) + sends_corner(k, 0) + sends_corner(k, 1))
+        return carry
+
+    def sent_exchange(k, carry):
+        query_copy(k).wait_send()
+        answer_copy(k).wait_send()
+        return carry
+
+    sent_all(sends_own())
+    lax.fori_loop(1, n_z, sent_line, 0)
+    lax.fori_loop(0, n_z, sent_rest, 0)
+    lax.fori_loop(1, n_usr, sent_exchange, 0)
+
+
+def fused_shards(
+    candidates, hist_kv, hist_len, block_mask, tile_user, tile_count, weight_in, weight_out
+):
+    row_total, model_width = candidates.shape
+    n_usr, n_grp = lax.axis_size("usr"), lax.axis_size("grp")
+    devices = n_usr * n_grp
+    depth, width = weight_in.shape
+    out_rows = weight_out.shape[0]
+    tiles = tile_user.shape[0]
+    tile_rows = row_total // tiles
+    sends = 6 + 3 * (n_usr // 2 - 1) + 6 * (n_usr // 2)
+    exchange = pltpu.VMEM((n_usr, HEADS, tile_rows, width), jnp.bfloat16)
+    dma = pltpu.SemaphoreType.DMA
+    in_vmem = pl.BlockSpec(memory_space=pltpu.VMEM)
+    in_smem = pl.BlockSpec(memory_space=pltpu.SMEM)
+    flops = 2 * row_total * model_width * model_width * 5 + 8 * n_usr * tile_rows * hist_kv.shape[1] * model_width
+    return pl.pallas_call(
+        functools.partial(layer_kernel, n_usr),
+        out_shape=jax.ShapeDtypeStruct((row_total, model_width), jnp.bfloat16),
+        in_specs=[in_vmem, in_vmem, in_smem, in_smem, in_smem, in_smem, in_vmem, in_vmem],
+        out_specs=in_vmem,
+        scratch_shapes=[
+            pltpu.VMEM((row_total, model_width), jnp.bfloat16),
+            pltpu.VMEM((devices, depth, width), jnp.bfloat16),
+            pltpu.VMEM((devices, out_rows, model_width), jnp.bfloat16),
+            pltpu.VMEM((devices, tiles, tile_rows, width), jnp.bfloat16),
+            pltpu.VMEM((HEADS, tiles, tile_rows, width), jnp.float32),
+            exchange,
+            exchange,
+            exchange,
+            exchange,
+            pltpu.VMEM((tiles, tile_rows, model_width), jnp.bfloat16),
+            dma((devices, 2)),
+            dma((devices, 2)),
+            dma((sends,)),
+            dma((sends,)),
+            dma((n_usr,)),
+            dma((n_usr,)),
+            dma((n_usr,)),
+            dma((n_usr,)),
+        ],
+        compiler_params=pltpu.CompilerParams(
+            collective_id=0, has_side_effects=True, vmem_limit_bytes=48 * 1024 * 1024
+        ),
+        cost_estimate=pl.CostEstimate(flops=flops, bytes_accessed=4 * 1024 * 1024, transcendentals=0),
+    )(candidates, hist_kv, hist_len, block_mask, tile_user, tile_count, weight_in, weight_out)
+
+
 def solution(mesh):
     in_specs = (
         P(("grp", "usr"), None),
@@ -117,4 +478,6 @@
         P(("grp", "usr"), None),
     )
     out_specs = P(("grp", "usr"), None)
-    return jax.shard_map(shards, mesh=mesh, in_specs=in_specs, out_specs=out_specs, check_vma=False)
+    fits = mesh.shape["grp"] == 4 and mesh.shape["usr"] == HEADS
+    body = fused_shards if fits else shards
+    return jax.shard_map(body, mesh=mesh, in_specs=in_specs, out_specs=out_specs, check_vma=False)

time: 206 us -> 135 us (0.66)
  waiting for transfers between devices: 150 us -> 0 us
  Pallas kernels: 0 us -> 126 us
  matrix products: 14.4 us -> 0 us
  between operations: 14.2 us -> 0.67 us
  starting transfers between devices: 7.66 us -> 0 us
  local copies, waits for them, and re-layouts: 13 us -> 7.08 us
  other arithmetic: 5.47 us -> 0 us
    pallas_call x0 -> x1, Pallas kernels: none -> 126 us  [fused_shards(): pl.pallas_call(functools.partial(layer_kernel, n_usr), out_shape=jax.Shap...]
    all_gather x2 -> x0, waiting for transfers between devices: 95.6 us -> none  [the longest x1 94.6 us: shards(): lax.all_gather(weight_in, ('grp', 'usr'), axis=1, tiled=True)]
    all_to_all x2 -> x0, waiting for transfers between devices: 52.6 us -> none  [the longest x1 30.6 us: shards(): lax.all_to_all(holder_attend(incoming, hist_keys, hist_values, live_items...]
    dot_general x3 -> x0, matrix products: 14.4 us -> none  [the longest x1 6.12 us: shards(): jnp.dot(normed, lax.all_gather(weight_in, ('grp', 'usr'), axis=1, tiled=T...]
    all_to_all x2 -> x0, starting transfers between devices: 7.62 us -> none  [the longest x1 4.06 us: shards(): lax.all_to_all(holder_attend(incoming, hist_keys, hist_values, live_items...]
    reduce_sum x5 -> x0, other arithmetic: 4.44 us -> none  [the longest x2 2.53 us: norm_rows(): centred = values_in - jnp.mean(values_in, axis=-1, keepdims=True)]
    unnamed x14, local copies, waits for them, and re-layouts: 3.36 us -> 7.08 us
    convert_element_type x2 -> x0, local copies, waits for them, and re-layouts: 3.35 us -> none  [answer_rows(): attend_rows(row_block, hist_keys, hist_values, live_items, score_scale)]
  transfers between devices with their start and end apart: 4 -> 0, of which waited for: 4 -> 0; matrix products, arithmetic and copies ran while one was open for 9% -> 0% of each run, Pallas kernels for 0% -> 0%
where the time goes in v1:
time: 135 us; the launch traced here: 134 us
  Pallas kernels  126 us (93%)
  local copies, waits for them, and re-layouts  7.08 us (5%)
    pallas_call x1, Pallas kernels, fused_shards(): pl.pallas_call(functools.partial(layer_kernel, n_usr), out_shape=jax.Shap...  126 us
    unnamed x14, local copies, waits for them, and re-layouts  7.08 us

profile of v1, /device:TPU:1, one launch (start us, length us, event | category | flops | bytes accessed | tf_op | source)
XLA Modules:
  0.0 134.1 jit_solution(14709171470310714433)
XLA Ops:
  0.7 0.7 copy.9.user_ref
  1.4 0.0 copy-start
  1.4 1.4 %copy-done = bf16[1,384,2048]{2,1,0:T(8,128)(2,1)S(1)} copy-done((bf16[1,384,2048]{2,1,0:T(8,128)(2,1)S(1)}, bf16[1,384,2048]{2,1,0:T(8,128)(2,1)}, u32[]{:S(2)}) %copy-start) | copy-done | bytes 1572888
  2.8 0.0 copy-start.1
  2.8 1.0 copy-done.1
  3.8 0.0 copy-start.2
  3.8 0.9 copy-done.2
  4.8 0.0 copy-start.3
  4.8 0.8 copy-done.3
  5.6 0.0 copy-start.4
  5.6 0.7 copy-done.4
  6.3 0.0 copy-start.5
  6.3 0.7 copy-done.5
  6.9 126.3 %shard_map.82 = bf16[256,1024]{1,0:T(8,128)(2,1)S(1)} custom-call(bf16[256,1024]{1,0:T(8,128)(2,1)S(1)} %copy-done.1, bf16[1,384,2048]{2,1,0:T(8,128)(2,1)S(1)} %copy-done, s32[1]{0:T(128)S(6)} %copy.11.len_ref, s32[1,3]{1,0:T(1,128)S(1)} %copy-done.4, s32[4,1]{1,0:T(4,128)S(1)} %copy.9.user_ref, s32[4]{0:T(128)S(1)} %copy-done.5, ...), custom_call_target="tpu_custom_call" | custom-call | flops 4294967296 | bytes 4194304 | tf_op jit(solution)/shard_map/pallas_call | solution.py:437
  133.3 0.8 copy.12
Async XLA Ops:
  1.4 1.4 %copy-start = (bf16[1,384,2048]{2,1,0:T(8,128)(2,1)S(1)}, bf16[1,384,2048]{2,1,0:T(8,128)(2,1)}, u32[]{:S(2)}) copy-start(bf16[1,384,2048]{2,1,0:T(8,128)(2,1)} %kv_ref.1) | copy-start | bytes 4718596
  2.8 1.0 copy-start.1
  3.8 0.9 copy-start.2
  4.8 0.8 copy-start.3
  5.6 0.7 copy-start.4
  6.3 0.7 copy-start.5

commit v2 on v1

--- a/solution.py
+++ b/solution.py
@@ -187,46 +187,89 @@
             device_id_type=MESH,
         )
 
+    is_query, x_is_query = (x == 0) & (c == 0), (x == 1) & (c == 0)
+    sib_is_query, diagonal_is_query = (x == 0) & (c == 1), (x == 1) & (c == 1)
+
+    def along_z(slot, zz, base):
+        up, down = (zz <= z) & (z + 1 < n_z), (zz >= z) & (z > 0)
+        return [
+            (up, slot, None, (g, (z + 1) * 2 + y), base),
+            (down, slot, None, (g, (z - 1) * 2 + y), base + 1),
+        ]
+
     def sends_own():
         me = slot_of(x, c, y, z)
-        listed = [(me, None, (g, ((z + k) % n_z) * 2 + y), k - 1) for k in range(1, n_z)]
-        return listed + [(me, None, to_x, 3), (me, None, to_y, 4), (me, None, to_c, 5)]
-
-    def sends_line(k):
-        slot = slot_of(x, c, y, (z + k) % n_z)
-        base = 6 + (k - 1) * 3
-        return [(slot, None, to_x, base), (slot, None, to_y, base + 1), (slot, None, to_c, base + 2)]
+        return along_z(me, z, 0) + [(None, me, None, to_y, 2), (None, me, None, to_c, 3)]
+
+    def sends_across():
+        return [(None, slot_of(x, c, y, z), None, to_x, 4)]
+
+    def sends_line(zz):
+        slot = slot_of(x, c, y, zz)
+        base = 5 + zz * 5
+        return along_z(slot, zz, base) + [
+            (None, slot, None, to_x, base + 2),
+            (None, slot, None, to_y, base + 3),
+            (None, slot, None, to_c, base + 4),
+        ]
 
     def sends_y(k):
         slot = slot_of(x, c, 1 - y, (z + k) % n_z)
-        base = 15 + k * 2
-        return [(slot, 0, to_x, base), (slot, None, to_c, base + 1)]
+        base = 5 + n_z * 5 + k * 2
+        return [(None, slot, 0, to_x, base), (None, slot, None, to_c, base + 1)]
 
     def sends_x(k):
         slot = slot_of(1 - x, c, y, (z + k) % n_z)
-        base = 23 + k * 2
-        return [(slot, 1, to_y, base), (slot, None, to_c, base + 1)]
+        base = 5 + n_z * 7 + k * 2
+        return [(None, slot, 1, to_y, base), (None, slot, None, to_c, base + 1)]
 
     def sends_corner(k, part):
         slot = slot_of(1 - x, c, 1 - y, (z + k) % n_z)
-        return [(slot, part, to_c, 31 + k * 2 + part)]
-
-    def start_all(copy, listed):
-        for entry in listed:
-            copy(*entry).start()
+        return [(None, slot, part, to_c, 5 + n_z * 9 + k * 2 + part)]
+
+    def sends_query(zz):
+        slot = slot_of(0, 0, y, zz)
+        base = 5 + n_z * 11 + zz * 4
+        return along_z(slot, zz, base) + [(None, slot, None, to_y, base + 2), (None, slot, None, to_c, base + 3)]
+
+    def sends_query_y(k):
+        slot = slot_of(0, 0, 1 - y, (z + k) % n_z)
+        return [(None, slot, None, to_c, 5 + n_z * 15 + k)]
+
+    def each(copy, listed, act):
+        for needed, slot, part, target, sem in listed:
+            if needed is None:
+                act(copy(slot, part, target, sem))
+            else:
+                pl.when(needed)(lambda a=(slot, part, target, sem): act(copy(*a)))
+
+    def start(descriptor):
+        descriptor.start()
+
+    def sent(descriptor):
+        descriptor.wait_send()
 
     def arrived(copy, slot, part):
         copy(slot, part, to_c, 0).wait_recv()
-
-    def relay(slot, part, listed):
-        arrived(w_copy, slot, part)
-        start_all(w_copy, listed)
-        arrived(o_copy, slot, part)
-        start_all(o_copy, listed)
 
     def project(slot):
         block = silu(jnp.dot(normed[...], w_all[slot], preferred_element_type=jnp.float32))
         proj[slot] = block.astype(jnp.bfloat16).reshape(tiles, tile_rows, width)
+
+    def relay(slot, parts, listed, skip):
+        @pl.when(jnp.logical_not(skip))
+        def _():
+            for part in parts:
+                arrived(w_copy, slot, part)
+                each(w_copy, [e for e in listed if len(parts) == 1 or e[2] == part], start)
+
+        for part in parts:
+            arrived(o_copy, slot, part)
+            each(o_copy, [e for e in listed if len(parts) == 1 or e[2] == part], start)
+
+        @pl.when(jnp.logical_not(skip))
+        def _():
+            project(slot)
 
     barrier = pltpu.get_barrier_semaphore()
     peers = [to_x, to_c] + [(g, (u + k) % n_usr) for k in range(1, n_usr)]
@@ -237,54 +280,47 @@
     wo_all[mine] = wout_ref[...]
     pl.semaphore_wait(barrier, len(peers))
 
-    start_all(w_copy, sends_own())
-    start_all(o_copy, sends_own())
+    each(w_copy, sends_across(), start)
+
+    def query_relay(zz, known):
+        slot = slot_of(0, 0, y, zz)
+
+        @pl.when(jnp.logical_not(known))
+        def _():
+            arrived(w_copy, slot, None)
+
+        @pl.when(c == 0)
+        def _():
+            each(w_copy, sends_query(zz), start)
+
+    query_relay(z, is_query)
     normed[...] = norm_rows(cand_ref[...].astype(jnp.float32)).astype(jnp.bfloat16)
-    project(mine)
-
-    def line_step(k, carry):
-        slot = slot_of(x, c, y, (z + k) % n_z)
-        relay(slot, None, sends_line(k))
+    project(slot_of(0, 0, y, z))
+
+    def query_line(k, carry):
+        for zz in (z - k, z + k):
+
+            @pl.when((zz >= 0) & (zz < n_z))
+            def _(zz=zz):
+                query_relay(zz, False)
+                project(slot_of(0, 0, y, zz))
+
+        return carry
+
+    lax.fori_loop(1, n_z, query_line, 0)
+
+    def query_side(k, carry):
+        slot = slot_of(0, 0, 1 - y, (z + k) % n_z)
+        arrived(w_copy, slot, None)
+
+        @pl.when(c == 0)
+        def _():
+            each(w_copy, sends_query_y(k), start)
+
         project(slot)
         return carry
 
-    lax.fori_loop(1, n_z, line_step, 0)
-
-    def take(slot, parts):
-        for part in parts:
-            arrived(w_copy, slot, part)
-            arrived(o_copy, slot, part)
-        project(slot)
-
-    def side_step(k, carry):
-        zz = (z + k) % n_z
-        slot_y, slot_x = slot_of(x, c, 1 - y, zz), slot_of(1 - x, c, y, zz)
-        relay(slot_y, None, sends_y(k))
-        relay(slot_x, None, sends_x(k))
-        project(slot_y)
-        project(slot_x)
-        take(slot_of(x, 1 - c, y, zz), (None,))
-        return carry
-
-    lax.fori_loop(0, n_z, side_step, 0)
-
-    def corner_step(k, carry):
-        zz = (z + k) % n_z
-        slot = slot_of(1 - x, c, 1 - y, zz)
-        for part in range(2):
-            relay(slot, part, sends_corner(k, part))
-        project(slot)
-        take(slot_of(x, 1 - c, 1 - y, zz), (None,))
-        take(slot_of(1 - x, 1 - c, y, zz), (None,))
-        return carry
-
-    lax.fori_loop(0, n_z, corner_step, 0)
-
-    def last_step(k, carry):
-        take(slot_of(1 - x, 1 - c, 1 - y, (z + k) % n_z), (0, 1))
-        return carry
-
-    lax.fori_loop(0, n_z, last_step, 0)
+    lax.fori_loop(0, n_z, query_side, 0)
 
     def query_copy(k):
         holder = (u + k) % n_usr
@@ -345,7 +381,60 @@
                 jnp.bfloat16
             )
 
+    @pl.when(jnp.logical_not(is_query))
+    def _():
+        each(w_copy, sends_own(), start)
+        project(mine)
+
+    each(o_copy, sends_own(), start)
+    each(o_copy, sends_across(), start)
+
     attend(u, returned)
+
+    def line_step(k, carry):
+        for zz in (z - k, z + k):
+
+            @pl.when((zz >= 0) & (zz < n_z))
+            def _(zz=zz):
+                relay(slot_of(x, c, y, zz), (None,), sends_line(zz), is_query)
+
+        return carry
+
+    lax.fori_loop(1, n_z, line_step, 0)
+
+    def side_step(k, carry):
+        zz = (z + k) % n_z
+        relay(slot_of(x, c, 1 - y, zz), (None,), sends_y(k), is_query)
+        relay(slot_of(1 - x, c, y, zz), (None,), sends_x(k), x_is_query)
+        relay(slot_of(x, 1 - c, y, zz), (None,), [], sib_is_query)
+        return carry
+
+    lax.fori_loop(0, n_z, side_step, 0)
+
+    def answer_step(k, carry):
+        query_copy(k).wait_recv()
+        attend((u + n_usr - k) % n_usr, answers)
+        answer_copy(k).start()
+        return carry
+
+    lax.fori_loop(1, n_usr, answer_step, 0)
+
+    def corner_step(k, carry):
+        zz = (z + k) % n_z
+        corner = sends_corner(k, 0) + sends_corner(k, 1)
+        relay(slot_of(1 - x, c, 1 - y, zz), (0, 1), corner, x_is_query)
+        relay(slot_of(x, 1 - c, 1 - y, zz), (None,), [], sib_is_query)
+        relay(slot_of(1 - x, 1 - c, y, zz), (None,), [], diagonal_is_query)
+        return carry
+
+    lax.fori_loop(0, n_z, corner_step, 0)
+
+    def last_step(k, carry):
+        slot = slot_of(1 - x, 1 - c, 1 - y, (z + k) % n_z)
+        relay(slot, (0, 1), [], diagonal_is_query)
+        return carry
+
+    lax.fori_loop(0, n_z, last_step, 0)
 
     def own_step(h, carry):
         queries = proj[h].astype(jnp.float32)
@@ -355,14 +444,6 @@
         return carry
 
     lax.fori_loop(0, HEADS, own_step, 0)
-
-    def answer_step(k, carry):
-        query_copy(k).wait_recv()
-        attend((u + n_usr - k) % n_usr, answers)
-        answer_copy(k).start()
-        return carry
-
-    lax.fori_loop(1, n_usr, answer_step, 0)
 
     def return_step(k, carry):
         answer_copy(k).wait_recv()
@@ -394,17 +475,40 @@
                 jnp.bfloat16
             )
 
-    def sent_all(listed):
-        for entry in listed:
-            w_copy(*entry).wait_send()
-            o_copy(*entry).wait_send()
-
-    def sent_line(k, carry):
-        sent_all(sends_line(k))
+    each(w_copy, sends_across(), sent)
+    each(o_copy, sends_own() + sends_across(), sent)
+
+    @pl.when(jnp.logical_not(is_query))
+    def _():
+        each(w_copy, sends_own(), sent)
+
+    def sent_line(zz, carry):
+        @pl.when(zz != z)
+        def _():
+            each(o_copy, sends_line(zz), sent)
+
+        @pl.when((zz != z) & jnp.logical_not(is_query))
+        def _():
+            each(w_copy, sends_line(zz), sent)
+
+        @pl.when(c == 0)
+        def _():
+            each(w_copy, sends_query(zz) + sends_query_y(zz), sent)
+
         return carry
 
     def sent_rest(k, carry):
-        sent_all(sends_y(k) + sends_x(k) + sends_corner(k, 0) + sends_corner(k, 1))
+        by_y, by_x = sends_y(k), sends_x(k) + sends_corner(k, 0) + sends_corner(k, 1)
+        each(o_copy, by_y + by_x, sent)
+
+        @pl.when(jnp.logical_not(is_query))
+        def _():
+            each(w_copy, by_y, sent)
+
+        @pl.when(jnp.logical_not(x_is_query))
+        def _():
+            each(w_copy, by_x, sent)
+
         return carry
 
     def sent_exchange(k, carry):
@@ -412,8 +516,7 @@
         answer_copy(k).wait_send()
         return carry
 
-    sent_all(sends_own())
-    lax.fori_loop(1, n_z, sent_line, 0)
+    lax.fori_loop(0, n_z, sent_line, 0)
     lax.fori_loop(0, n_z, sent_rest, 0)
     lax.fori_loop(1, n_usr, sent_exchange, 0)
 
@@ -428,7 +531,7 @@
     out_rows = weight_out.shape[0]
     tiles = tile_user.shape[0]
     tile_rows = row_total // tiles
-    sends = 6 + 3 * (n_usr // 2 - 1) + 6 * (n_usr // 2)
+    sends = 5 + 16 * (n_usr // 2)
     exchange = pltpu.VMEM((n_usr, HEADS, tile_rows, width), jnp.bfloat16)
     dma = pltpu.SemaphoreType.DMA
     in_vmem = pl.BlockSpec(memory_space=pltpu.VMEM)
@@ -453,7 +556,7 @@
             dma((devices, 2)),
             dma((devices, 2)),
             dma((sends,)),
-            dma((sends,)),
+            dma((5 + 11 * (n_usr // 2),)),
             dma((n_usr,)),
             dma((n_usr,)),
             dma((n_usr,)),

time: 135 us -> 127 us (0.941)
  Pallas kernels: 126 us -> 117 us
    pallas_call x1, Pallas kernels: 126 us -> 117 us  [fused_shards(): pl.pallas_call(functools.partial(layer_kernel, n_usr), out_shape=jax.Shap...]
where the time goes in v2:
time: 127 us; the launch traced here: 125 us
  Pallas kernels  117 us (92%)
  local copies, waits for them, and re-layouts  7.08 us (6%)
    pallas_call x1, Pallas kernels, fused_shards(): pl.pallas_call(functools.partial(layer_kernel, n_usr), out_shape=jax.Shap...  117 us
    unnamed x14, local copies, waits for them, and re-layouts  7.08 us

profile of v2, /device:TPU:1, one launch (start us, length us, event | category | flops | bytes accessed | tf_op | source)
XLA Modules:
  0.0 125.2 jit_solution(2641666024749241415)
XLA Ops:
  0.7 0.7 copy.9.user_ref
  1.4 0.0 copy-start
  1.4 1.4 %copy-done = bf16[1,384,2048]{2,1,0:T(8,128)(2,1)S(1)} copy-done((bf16[1,384,2048]{2,1,0:T(8,128)(2,1)S(1)}, bf16[1,384,2048]{2,1,0:T(8,128)(2,1)}, u32[]{:S(2)}) %copy-start) | copy-done | bytes 1572888
  2.8 0.0 copy-start.1
  2.8 1.0 copy-done.1
  3.8 0.0 copy-start.2
  3.8 0.9 copy-done.2
  4.8 0.0 copy-start.3
  4.8 0.8 copy-done.3
  5.6 0.0 copy-start.4
  5.6 0.7 copy-done.4
  6.3 0.0 copy-start.5
  6.3 0.7 copy-done.5
  6.9 117.4 %shard_map.82 = bf16[256,1024]{1,0:T(8,128)(2,1)S(1)} custom-call(bf16[256,1024]{1,0:T(8,128)(2,1)S(1)} %copy-done.1, bf16[1,384,2048]{2,1,0:T(8,128)(2,1)S(1)} %copy-done, s32[1]{0:T(128)S(6)} %copy.11.len_ref, s32[1,3]{1,0:T(1,128)S(1)} %copy-done.4, s32[4,1]{1,0:T(4,128)S(1)} %copy.9.user_ref, s32[4]{0:T(128)S(1)} %copy-done.5, ...), custom_call_target="tpu_custom_call" | custom-call | flops 4294967296 | bytes 4194304 | tf_op jit(solution)/shard_map/pallas_call | solution.py:540
  124.4 0.8 copy.12
Async XLA Ops:
  1.4 1.4 %copy-start = (bf16[1,384,2048]{2,1,0:T(8,128)(2,1)S(1)}, bf16[1,384,2048]{2,1,0:T(8,128)(2,1)}, u32[]{:S(2)}) copy-start(bf16[1,384,2048]{2,1,0:T(8,128)(2,1)} %kv_ref.1) | copy-start | bytes 4718596
  2.8 1.0 copy-start.1
  3.8 0.9 copy-start.2
  4.8 0.8 copy-start.3
  5.6 0.7 copy-start.4
  6.3 0.7 copy-start.5

commit v3 on v2

--- a/solution.py
+++ b/solution.py
@@ -110,20 +110,24 @@
 
 
 def silu(v):
-    return v / (1.0 + jnp.exp(-v))
+    half = 0.5 * v
+    return half + half * jnp.tanh(half)
 
 
 def layer_kernel(
     n_usr,
-    cand_ref,
-    kv_ref,
+    cand_hbm,
+    kv_hbm,
     len_ref,
     mask_ref,
     user_ref,
     count_ref,
-    win_ref,
-    wout_ref,
+    win_hbm,
+    wout_hbm,
     out_ref,
+    cand_ref,
+    kv_ref,
+    key_heads,
     normed,
     w_all,
     wo_all,
@@ -142,9 +146,10 @@
     q_send,
     a_recv,
     a_send,
+    load_sem,
 ):
-    depth, width = win_ref.shape
-    out_rows = wout_ref.shape[0]
+    depth, width = win_hbm.shape
+    out_rows = wout_hbm.shape[0]
     row_total, model_width = cand_ref.shape
     tiles = user_ref.shape[0]
     tile_rows = row_total // tiles
@@ -204,6 +209,9 @@
     def sends_across():
         return [(None, slot_of(x, c, y, z), None, to_x, 4)]
 
+    def sends_query_across():
+        return [(None, slot_of(0, 0, y, z), part, to_x, 5 + n_z * 11 + part) for part in range(2)]
+
     def sends_line(zz):
         slot = slot_of(x, c, y, zz)
         base = 5 + zz * 5
@@ -227,14 +235,20 @@
         slot = slot_of(1 - x, c, 1 - y, (z + k) % n_z)
         return [(None, slot, part, to_c, 5 + n_z * 9 + k * 2 + part)]
 
-    def sends_query(zz):
+    def sends_query(zz, part):
         slot = slot_of(0, 0, y, zz)
-        base = 5 + n_z * 11 + zz * 4
-        return along_z(slot, zz, base) + [(None, slot, None, to_y, base + 2), (None, slot, None, to_c, base + 3)]
-
-    def sends_query_y(k):
+        base = 7 + n_z * 11 + zz * 8 + part * 4
+        up, down = (zz <= z) & (z + 1 < n_z), (zz >= z) & (z > 0)
+        return [
+            (up, slot, part, (g, (z + 1) * 2 + y), base),
+            (down, slot, part, (g, (z - 1) * 2 + y), base + 1),
+            (None, slot, part, to_y, base + 2),
+            (None, slot, part, to_c, base + 3),
+        ]
+
+    def sends_query_y(k, part):
         slot = slot_of(0, 0, 1 - y, (z + k) % n_z)
-        return [(None, slot, None, to_c, 5 + n_z * 15 + k)]
+        return [(None, slot, part, to_c, 7 + n_z * 19 + k * 2 + part)]
 
     def each(copy, listed, act):
         for needed, slot, part, target, sem in listed:
@@ -276,25 +290,41 @@
     for peer in peers:
         pl.semaphore_signal(barrier, inc=1, device_id=peer, device_id_type=MESH)
     mine = slot_of(x, c, y, z)
-    w_all[mine] = win_ref[...]
-    wo_all[mine] = wout_ref[...]
+    loads = [
+        pltpu.make_async_copy(cand_hbm, cand_ref, load_sem.at[0]),
+        pltpu.make_async_copy(win_hbm, w_all.at[mine], load_sem.at[1]),
+        pltpu.make_async_copy(wout_hbm, wo_all.at[mine], load_sem.at[2]),
+        pltpu.make_async_copy(kv_hbm, kv_ref, load_sem.at[3]),
+    ]
+    for load in loads:
+        load.start()
+    loads[0].wait()
+    normed[...] = norm_rows(cand_ref[...].astype(jnp.float32)).astype(jnp.bfloat16)
+    loads[1].wait()
     pl.semaphore_wait(barrier, len(peers))
 
-    each(w_copy, sends_across(), start)
+    @pl.when(is_query)
+    def _():
+        each(w_copy, sends_query_across(), start)
+
+    @pl.when(jnp.logical_not(is_query))
+    def _():
+        each(w_copy, sends_across(), start)
 
     def query_relay(zz, known):
         slot = slot_of(0, 0, y, zz)
 
-        @pl.when(jnp.logical_not(known))
-        def _():
-            arrived(w_copy, slot, None)
-
-        @pl.when(c == 0)
-        def _():
-            each(w_copy, sends_query(zz), start)
+        for part in range(2):
+
+            @pl.when(jnp.logical_not(known))
+            def _(part=part):
+                arrived(w_copy, slot, part)
+
+            @pl.when(c == 0)
+            def _(part=part):
+                each(w_copy, sends_query(zz, part), start)
 
     query_relay(z, is_query)
-    normed[...] = norm_rows(cand_ref[...].astype(jnp.float32)).astype(jnp.bfloat16)
     project(slot_of(0, 0, y, z))
 
     def query_line(k, carry):
@@ -311,11 +341,12 @@
 
     def query_side(k, carry):
         slot = slot_of(0, 0, 1 - y, (z + k) % n_z)
-        arrived(w_copy, slot, None)
-
-        @pl.when(c == 0)
-        def _():
-            each(w_copy, sends_query_y(k), start)
+        for part in range(2):
+            arrived(w_copy, slot, part)
+
+            @pl.when(c == 0)
+            def _(part=part):
+                each(w_copy, sends_query_y(k, part), start)
 
         project(slot)
         return carry
@@ -323,7 +354,7 @@
     lax.fori_loop(0, n_z, query_side, 0)
 
     def query_copy(k):
-        holder = (u + k) % n_usr
+        holder = ((z + k // 2) % n_z) * 2 + (y + k) % 2
         return pltpu.make_async_remote_copy(
             src_ref=outgoing.at[holder],
             dst_ref=incoming.at[u],
@@ -333,8 +364,11 @@
             device_id_type=MESH,
         )
 
+    def source_of(k):
+        return ((z + n_z - k // 2) % n_z) * 2 + (y + k) % 2
+
     def answer_copy(k):
-        source = (u + n_usr - k) % n_usr
+        source = source_of(k)
         return pltpu.make_async_remote_copy(
             src_ref=answers.at[source],
             dst_ref=returned.at[u],
@@ -351,7 +385,7 @@
         return chosen
 
     def dispatch_step(k, carry):
-        holder = (u + k) % n_usr
+        holder = ((z + k // 2) % n_z) * 2 + (y + k) % 2
         tile = tile_for(holder)
         for h in range(HEADS):
             outgoing[holder, h] = proj[h, tile]
@@ -369,25 +403,31 @@
         kept = jnp.where(positions // BLK == b, mask_ref[0, b], kept)
     live = jnp.where((positions < len_ref[0]) & (kept > 0), 1.0, 0.0)
 
+    loads[3].wait()
+    for h in range(HEADS):
+        key_heads[h] = kv_ref[0, :, h * width : (h + 1) * width].T
+
     def attend(slot, dest):
         for h in range(HEADS):
-            keys = kv_ref[0, :, h * width : (h + 1) * width]
             values = kv_ref[0, :, model_width + h * width : model_width + (h + 1) * width]
-            scores = lax.dot_general(
-                incoming[slot, h], keys, (((1,), (1,)), ((), ())), preferred_element_type=jnp.float32
-            )
+            scores = jnp.dot(incoming[slot, h], key_heads[h], preferred_element_type=jnp.float32)
             weights = (silu(scores * scale) * live).astype(jnp.bfloat16)
             dest[slot, h] = jnp.dot(weights, values, preferred_element_type=jnp.float32).astype(
                 jnp.bfloat16
             )
 
+    def answer(k):
+        query_copy(k).wait_recv()
+        attend(source_of(k), answers)
+        answer_copy(k).start()
+
     @pl.when(jnp.logical_not(is_query))
     def _():
         each(w_copy, sends_own(), start)
         project(mine)
 
-    each(o_copy, sends_own(), start)
-    each(o_copy, sends_across(), start)
+    loads[2].wait()
+    each(o_copy, sends_own() + sends_across(), start)
 
     attend(u, returned)
 
@@ -398,6 +438,7 @@
             def _(zz=zz):
                 relay(slot_of(x, c, y, zz), (None,), sends_line(zz), is_query)
 
+        answer(k)
         return carry
 
     lax.fori_loop(1, n_z, line_step, 0)
@@ -407,17 +448,10 @@
         relay(slot_of(x, c, 1 - y, zz), (None,), sends_y(k), is_query)
         relay(slot_of(1 - x, c, y, zz), (None,), sends_x(k), x_is_query)
         relay(slot_of(x, 1 - c, y, zz), (None,), [], sib_is_query)
+        answer(n_z + k)
         return carry
 
     lax.fori_loop(0, n_z, side_step, 0)
-
-    def answer_step(k, carry):
-        query_copy(k).wait_recv()
-        attend((u + n_usr - k) % n_usr, answers)
-        answer_copy(k).start()
-        return carry
-
-    lax.fori_loop(1, n_usr, answer_step, 0)
 
     def corner_step(k, carry):
         zz = (z + k) % n_z
@@ -475,12 +509,15 @@
                 jnp.bfloat16
             )
 
-    each(w_copy, sends_across(), sent)
+    @pl.when(is_query)
+    def _():
+        each(w_copy, sends_query_across(), sent)
+
     each(o_copy, sends_own() + sends_across(), sent)
 
     @pl.when(jnp.logical_not(is_query))
     def _():
-        each(w_copy, sends_own(), sent)
+        each(w_copy, sends_own() + sends_across(), sent)
 
     def sent_line(zz, carry):
         @pl.when(zz != z)
@@ -493,7 +530,8 @@
 
         @pl.when(c == 0)
         def _():
-            each(w_copy, sends_query(zz) + sends_query_y(zz), sent)
+            for part in range(2):
+                each(w_copy, sends_query(zz, part) + sends_query_y(zz, part), sent)
 
         return carry
 
@@ -531,18 +569,22 @@
     out_rows = weight_out.shape[0]
     tiles = tile_user.shape[0]
     tile_rows = row_total // tiles
-    sends = 5 + 16 * (n_usr // 2)
+    sends = 7 + 21 * (n_usr // 2)
     exchange = pltpu.VMEM((n_usr, HEADS, tile_rows, width), jnp.bfloat16)
     dma = pltpu.SemaphoreType.DMA
+    in_any = pl.BlockSpec(memory_space=pl.ANY)
     in_vmem = pl.BlockSpec(memory_space=pltpu.VMEM)
     in_smem = pl.BlockSpec(memory_space=pltpu.SMEM)
     flops = 2 * row_total * model_width * model_width * 5 + 8 * n_usr * tile_rows * hist_kv.shape[1] * model_width
     return pl.pallas_call(
         functools.partial(layer_kernel, n_usr),
         out_shape=jax.ShapeDtypeStruct((row_total, model_width), jnp.bfloat16),
-        in_specs=[in_vmem, in_vmem, in_smem, in_smem, in_smem, in_smem, in_vmem, in_vmem],
+        in_specs=[in_any, in_any, in_smem, in_smem, in_smem, in_smem, in_any, in_any],
         out_specs=in_vmem,
         scratch_shapes=[
+            pltpu.VMEM((row_total, model_width), jnp.bfloat16),
+            pltpu.VMEM(hist_kv.shape, jnp.bfloat16),
+            pltpu.VMEM((HEADS, width, hist_kv.shape[1]), jnp.bfloat16),
             pltpu.VMEM((row_total, model_width), jnp.bfloat16),
             pltpu.VMEM((devices, depth, width), jnp.bfloat16),
             pltpu.VMEM((devices, out_rows, model_width), jnp.bfloat16),
@@ -561,9 +603,10 @@
             dma((n_usr,)),
             dma((n_usr,)),
             dma((n_usr,)),
+            dma((4,)),
         ],
         compiler_params=pltpu.CompilerParams(
-            collective_id=0, has_side_effects=True, vmem_limit_bytes=48 * 1024 * 1024
+            collective_id=0, has_side_effects=True, vmem_limit_bytes=60 * 1024 * 1024
         ),
         cost_estimate=pl.CostEstimate(flops=flops, bytes_accessed=4 * 1024 * 1024, transcendentals=0),
     )(candidates, hist_kv, hist_len, block_mask, tile_user, tile_count, weight_in, weight_out)

time: 127 us -> 110 us (0.87); the launches traced: 125 us -> 110 us
  Pallas kernels: 117 us -> 106 us
  local copies, waits for them, and re-layouts: 7.08 us -> 3.18 us
    pallas_call x1, Pallas kernels: 117 us -> 106 us  [fused_shards(): pl.pallas_call(functools.partial(layer_kernel, n_usr), out_shape=jax.Shap...]
    unnamed x14 -> x2, local copies, waits for them, and re-layouts: 7.08 us -> 3.18 us
where the time goes in v3:
time: 110 us
  Pallas kernels  106 us (96%)
  local copies, waits for them, and re-layouts  3.18 us (3%)
    pallas_call x1, Pallas kernels, fused_shards(): pl.pallas_call(functools.partial(layer_kernel, n_usr), out_shape=jax.Shap...  106 us
    unnamed x2, local copies, waits for them, and re-layouts  3.18 us

profile of v3, /device:TPU:1, one launch (start us, length us, event | category | flops | bytes accessed | tf_op | source)
XLA Modules:
  0.0 109.9 jit_solution(14807142573867811537)
XLA Ops:
  0.7 1.3 %copy.9.user_ref = s32[4,1]{1,0:T(4,128)} copy(s32[4,1]{0,1:T(1,128)} %param.12) | data formatting | bytes 32 | tf_op args[4]
  2.0 106.0 %shard_map.82 = bf16[256,1024]{1,0:T(8,128)(2,1)} custom-call(bf16[256,1024]{1,0:T(8,128)(2,1)} %cand_hbm.1, bf16[1,384,2048]{2,1,0:T(8,128)(2,1)} %kv_hbm.1, s32[1]{0:T(128)S(6)} %copy.11.len_ref, s32[1,3]{1,0:T(1,128)} %mask_ref.1, s32[4,1]{1,0:T(4,128)} %copy.9.user_ref, s32[4]{0:T(128)} %count_ref.1, bf16[1024,128]{1,0:T(8,128)(2,1)} %win_hbm.1, ...), custom_call_target="tpu_custom_call" | custom-call | flops 4294967296 | bytes 4194304 | tf_op jit(solution)/shard_map/pallas_call | solution.py:579
  108.0 1.9 %copy.12 = bf16[256,1024]{1,0:T(8,128)(2,1)} copy(bf16[256,1024]{1,0:T(8,128)(2,1)} %shard_map.82) | data formatting | bytes 1048576

commit v4 on v3

--- a/solution.py
+++ b/solution.py
@@ -151,7 +151,7 @@
     depth, width = win_hbm.shape
     out_rows = wout_hbm.shape[0]
     row_total, model_width = cand_ref.shape
-    tiles = user_ref.shape[0]
+    tiles = user_ref.shape[1]
     tile_rows = row_total // tiles
     items = kv_ref.shape[1]
     scale = width ** (-0.5)
@@ -180,14 +180,12 @@
         )
 
     def o_copy(slot, part, target, sem):
-        half = out_rows // 2
-        lo, size = (0, out_rows) if part is None else (part * half, half)
-        view = wo_all.at[slot, pl.ds(lo, size), :]
+        view = wo_all.at[slot]
         return pltpu.make_async_remote_copy(
             src_ref=view,
             dst_ref=view,
             send_sem=o_send.at[sem],
-            recv_sem=o_recv.at[slot, part or 0],
+            recv_sem=o_recv.at[slot],
             device_id=target,
             device_id_type=MESH,
         )
@@ -208,9 +206,6 @@
 
     def sends_across():
         return [(None, slot_of(x, c, y, z), None, to_x, 4)]
-
-    def sends_query_across():
-        return [(None, slot_of(0, 0, y, z), part, to_x, 5 + n_z * 11 + part) for part in range(2)]
 
     def sends_line(zz):
         slot = slot_of(x, c, y, zz)
@@ -224,31 +219,31 @@
     def sends_y(k):
         slot = slot_of(x, c, 1 - y, (z + k) % n_z)
         base = 5 + n_z * 5 + k * 2
-        return [(None, slot, 0, to_x, base), (None, slot, None, to_c, base + 1)]
+        return [(None, slot, None, to_x, base), (None, slot, None, to_c, base + 1)]
 
     def sends_x(k):
         slot = slot_of(1 - x, c, y, (z + k) % n_z)
-        base = 5 + n_z * 7 + k * 2
-        return [(None, slot, 1, to_y, base), (None, slot, None, to_c, base + 1)]
-
-    def sends_corner(k, part):
+        return [(None, slot, None, to_c, 5 + n_z * 7 + k)]
+
+    def sends_corner(k):
         slot = slot_of(1 - x, c, 1 - y, (z + k) % n_z)
-        return [(None, slot, part, to_c, 5 + n_z * 9 + k * 2 + part)]
+        return [(None, slot, None, to_c, 5 + n_z * 8 + k)]
 
     def sends_query(zz, part):
         slot = slot_of(0, 0, y, zz)
-        base = 7 + n_z * 11 + zz * 8 + part * 4
-        up, down = (zz <= z) & (z + 1 < n_z), (zz >= z) & (z > 0)
+        base = 5 + n_z * 9 + zz * 10 + part * 5
+        up, down = (x == 0) & (zz <= z) & (z + 1 < n_z), (x == 0) & (zz >= z) & (z > 0)
         return [
             (up, slot, part, (g, (z + 1) * 2 + y), base),
             (down, slot, part, (g, (z - 1) * 2 + y), base + 1),
-            (None, slot, part, to_y, base + 2),
-            (None, slot, part, to_c, base + 3),
+            (x == 0, slot, part, to_x, base + 2),
+            (None, slot, part, to_y, base + 3),
+            (None, slot, part, to_c, base + 4),
         ]
 
     def sends_query_y(k, part):
         slot = slot_of(0, 0, 1 - y, (z + k) % n_z)
-        return [(None, slot, part, to_c, 7 + n_z * 19 + k * 2 + part)]
+        return [(None, slot, part, to_c, 5 + n_z * 19 + k * 2 + part)]
 
     def each(copy, listed, act):
         for needed, slot, part, target, sem in listed:
@@ -270,16 +265,14 @@
         block = silu(jnp.dot(normed[...], w_all[slot], preferred_element_type=jnp.float32))
         proj[slot] = block.astype(jnp.bfloat16).reshape(tiles, tile_rows, width)
 
-    def relay(slot, parts, listed, skip):
+    def relay(slot, listed, skip):
         @pl.when(jnp.logical_not(skip))
         def _():
-            for part in parts:
-                arrived(w_copy, slot, part)
-                each(w_copy, [e for e in listed if len(parts) == 1 or e[2] == part], start)
-
-        for part in parts:
-            arrived(o_copy, slot, part)
-            each(o_copy, [e for e in listed if len(parts) == 1 or e[2] == part], start)
+            arrived(w_copy, slot, None)
+            each(w_copy, listed, start)
+
+        arrived(o_copy, slot, None)
+        each(o_copy, listed, start)
 
         @pl.when(jnp.logical_not(skip))
         def _():
@@ -303,10 +296,6 @@
     loads[1].wait()
     pl.semaphore_wait(barrier, len(peers))
 
-    @pl.when(is_query)
-    def _():
-        each(w_copy, sends_query_across(), start)
-
     @pl.when(jnp.logical_not(is_query))
     def _():
         each(w_copy, sends_across(), start)
@@ -381,7 +370,7 @@
     def tile_for(holder):
         chosen = 0
         for t in range(tiles):
-            chosen = jnp.where(user_ref[t, 0] == holder, t, chosen)
+            chosen = jnp.where(user_ref[0, t] == holder, t, chosen)
         return chosen
 
     def dispatch_step(k, carry):
@@ -436,7 +425,7 @@
 
             @pl.when((zz >= 0) & (zz < n_z))
             def _(zz=zz):
-                relay(slot_of(x, c, y, zz), (None,), sends_line(zz), is_query)
+                relay(slot_of(x, c, y, zz), sends_line(zz), is_query)
 
         answer(k)
         return carry
@@ -445,9 +434,9 @@
 
     def side_step(k, carry):
         zz = (z + k) % n_z
-        relay(slot_of(x, c, 1 - y, zz), (None,), sends_y(k), is_query)
-        relay(slot_of(1 - x, c, y, zz), (None,), sends_x(k), x_is_query)
-        relay(slot_of(x, 1 - c, y, zz), (None,), [], sib_is_query)
+        relay(slot_of(x, c, 1 - y, zz), sends_y(k), is_query)
+        relay(slot_of(1 - x, c, y, zz), sends_x(k), x_is_query)
+        relay(slot_of(x, 1 - c, y, zz), [], sib_is_query)
         answer(n_z + k)
         return carry
 
@@ -455,17 +444,16 @@
 
     def corner_step(k, carry):
         zz = (z + k) % n_z
-        corner = sends_corner(k, 0) + sends_corner(k, 1)
-        relay(slot_of(1 - x, c, 1 - y, zz), (0, 1), corner, x_is_query)
-        relay(slot_of(x, 1 - c, 1 - y, zz), (None,), [], sib_is_query)
-        relay(slot_of(1 - x, 1 - c, y, zz), (None,), [], diagonal_is_query)
+        relay(slot_of(1 - x, c, 1 - y, zz), sends_corner(k), x_is_query)
+        relay(slot_of(x, 1 - c, 1 - y, zz), [], sib_is_query)
+        relay(slot_of(1 - x, 1 - c, y, zz), [], diagonal_is_query)
         return carry
 
     lax.fori_loop(0, n_z, corner_step, 0)
 
     def last_step(k, carry):
         slot = slot_of(1 - x, 1 - c, 1 - y, (z + k) % n_z)
-        relay(slot, (0, 1), [], diagonal_is_query)
+        relay(slot, [], diagonal_is_query)
         return carry
 
     lax.fori_loop(0, n_z, last_step, 0)
@@ -486,7 +474,7 @@
     lax.fori_loop(1, n_usr, return_step, 0)
 
     def tile_step(t, carry):
-        holder = user_ref[t, 0]
+        holder = user_ref[0, t]
         combined = jnp.concatenate(
             [returned[holder, h].astype(jnp.float32) + own[h, t] for h in range(HEADS)], axis=-1
         )
@@ -509,10 +497,6 @@
                 jnp.bfloat16
             )
 
-    @pl.when(is_query)
-    def _():
-        each(w_copy, sends_query_across(), sent)
-
     each(o_copy, sends_own() + sends_across(), sent)
 
     @pl.when(jnp.logical_not(is_query))
@@ -536,7 +520,7 @@
         return carry
 
     def sent_rest(k, carry):
-        by_y, by_x = sends_y(k), sends_x(k) + sends_corner(k, 0) + sends_corner(k, 1)
+        by_y, by_x = sends_y(k), sends_x(k) + sends_corner(k)
         each(o_copy, by_y + by_x, sent)
 
         @pl.when(jnp.logical_not(is_query))
@@ -569,7 +553,7 @@
     out_rows = weight_out.shape[0]
     tiles = tile_user.shape[0]
     tile_rows = row_total // tiles
-    sends = 7 + 21 * (n_usr // 2)
+    sends = 5 + 21 * (n_usr // 2)
     exchange = pltpu.VMEM((n_usr, HEADS, tile_rows, width), jnp.bfloat16)
     dma = pltpu.SemaphoreType.DMA
     in_any = pl.BlockSpec(memory_space=pl.ANY)
@@ -596,9 +580,9 @@
             exchange,
             pltpu.VMEM((tiles, tile_rows, model_width), jnp.bfloat16),
             dma((devices, 2)),
-            dma((devices, 2)),
+            dma((devices,)),
             dma((sends,)),
-            dma((5 + 11 * (n_usr // 2),)),
+            dma((5 + 9 * (n_usr // 2),)),
             dma((n_usr,)),
             dma((n_usr,)),
             dma((n_usr,)),
@@ -609,7 +593,7 @@
             collective_id=0, has_side_effects=True, vmem_limit_bytes=60 * 1024 * 1024
         ),
         cost_estimate=pl.CostEstimate(flops=flops, bytes_accessed=4 * 1024 * 1024, transcendentals=0),
-    )(candidates, hist_kv, hist_len, block_mask, tile_user, tile_count, weight_in, weight_out)
+    )(candidates, hist_kv, hist_len, block_mask, tile_user.T, tile_count, weight_in, weight_out)
 
 
 def solution(mesh):

time: 110 us -> 119 us (1.082)
  Pallas kernels: 106 us -> 117 us
  local copies, waits for them, and re-layouts: 3.18 us -> 1.87 us
    pallas_call x1, Pallas kernels: 106 us -> 117 us  [fused_shards(): pl.pallas_call(functools.partial(layer_kernel, n_usr), out_shape=jax.Shap...]
    unnamed x2 -> x1, local copies, waits for them, and re-layouts: 3.18 us -> 1.87 us
where the time goes in v4:
time: 119 us
  Pallas kernels  117 us (98%)
  local copies, waits for them, and re-layouts  1.87 us (2%)
    pallas_call x1, Pallas kernels, fused_shards(): pl.pallas_call(functools.partial(layer_kernel, n_usr), out_shape=jax.Shap...  117 us

profile of v4, /device:TPU:1, one launch (start us, length us, event | category | flops | bytes accessed | tf_op | source)
XLA Modules:
  0.0 119.3 jit_solution(8765888849355564311)
XLA Ops:
  0.7 116.8 %shard_map.82 = bf16[256,1024]{1,0:T(8,128)(2,1)} custom-call(bf16[256,1024]{1,0:T(8,128)(2,1)} %cand_hbm.1, bf16[1,384,2048]{2,1,0:T(8,128)(2,1)} %kv_hbm.1, s32[1]{0:T(128)S(6)} %copy.10.len_ref, s32[1,3]{1,0:T(1,128)} %mask_ref.1, s32[1,4]{1,0:T(1,128)} %bitcast.1, s32[4]{0:T(128)} %count_ref.1, bf16[1024,128]{1,0:T(8,128)(2,1)} %win_hbm.1, ...), custom_call_target="tpu_custom_call" | custom-call | flops 4294967296 | bytes 4194304 | tf_op jit(solution)/shard_map/pallas_call | solution.py:563
  117.4 1.9 %copy.11 = bf16[256,1024]{1,0:T(8,128)(2,1)} copy(bf16[256,1024]{1,0:T(8,128)(2,1)} %shard_map.82) | data formatting | bytes 1048576

commit v5 on v4

--- a/solution.py
+++ b/solution.py
@@ -245,6 +245,14 @@
         slot = slot_of(0, 0, 1 - y, (z + k) % n_z)
         return [(None, slot, part, to_c, 5 + n_z * 19 + k * 2 + part)]
 
+    early, late = x == 1, (x == 0) & (c == 1)
+
+    def not_y(listed):
+        return [entry for entry in listed if entry[3] is not to_y]
+
+    def only_y(listed):
+        return [entry for entry in listed if entry[3] is to_y]
+
     def each(copy, listed, act):
         for needed, slot, part, target, sem in listed:
             if needed is None:
@@ -296,9 +304,9 @@
     loads[1].wait()
     pl.semaphore_wait(barrier, len(peers))
 
-    @pl.when(jnp.logical_not(is_query))
+    @pl.when(early)
     def _():
-        each(w_copy, sends_across(), start)
+        each(w_copy, sends_across() + not_y(sends_own()), start)
 
     def query_relay(zz, known):
         slot = slot_of(0, 0, y, zz)
@@ -323,6 +331,13 @@
             def _(zz=zz):
                 query_relay(zz, False)
                 project(slot_of(0, 0, y, zz))
+
+            @pl.when((zz >= 0) & (zz < n_z) & early)
+            def _(zz=zz):
+                slot = slot_of(x, c, y, zz)
+                arrived(w_copy, slot, None)
+                each(w_copy, not_y(sends_line(zz)), start)
+                project(slot)
 
         return carry
 
@@ -410,9 +425,25 @@
         attend(source_of(k), answers)
         answer_copy(k).start()
 
+    @pl.when(late)
+    def _():
+        each(w_copy, sends_own() + sends_across(), start)
+
+    @pl.when(early)
+    def _():
+        each(w_copy, only_y(sends_own()), start)
+
+    def line_y(zz, carry):
+        @pl.when(early & (zz != z))
+        def _():
+            each(w_copy, only_y(sends_line(zz)), start)
+
+        return carry
+
+    lax.fori_loop(0, n_z, line_y, 0)
+
     @pl.when(jnp.logical_not(is_query))
     def _():
-        each(w_copy, sends_own(), start)
         project(mine)
 
     loads[2].wait()
@@ -425,7 +456,7 @@
 
             @pl.when((zz >= 0) & (zz < n_z))
             def _(zz=zz):
-                relay(slot_of(x, c, y, zz), sends_line(zz), is_query)
+                relay(slot_of(x, c, y, zz), sends_line(zz), jnp.logical_not(late))
 
         answer(k)
         return carry

time: 119 us -> 117 us (0.983)
  Pallas kernels: 117 us -> 114 us
    pallas_call x1, Pallas kernels: 117 us -> 114 us  [fused_shards(): pl.pallas_call(functools.partial(layer_kernel, n_usr), out_shape=jax.Shap...]
where the time goes in v5:
time: 117 us; the launch traced here: 116 us
  Pallas kernels  114 us (97%)
  local copies, waits for them, and re-layouts  1.87 us (2%)
    pallas_call x1, Pallas kernels, fused_shards(): pl.pallas_call(functools.partial(layer_kernel, n_usr), out_shape=jax.Shap...  114 us

profile of v5, /device:TPU:1, one launch (start us, length us, event | category | flops | bytes accessed | tf_op | source)
XLA Modules:
  0.0 116.1 jit_solution(1847138721334030733)
XLA Ops:
  0.7 113.6 %shard_map.82 = bf16[256,1024]{1,0:T(8,128)(2,1)} custom-call(bf16[256,1024]{1,0:T(8,128)(2,1)} %cand_hbm.1, bf16[1,384,2048]{2,1,0:T(8,128)(2,1)} %kv_hbm.1, s32[1]{0:T(128)S(6)} %copy.10.len_ref, s32[1,3]{1,0:T(1,128)} %mask_ref.1, s32[1,4]{1,0:T(1,128)} %bitcast.1, s32[4]{0:T(128)} %count_ref.1, bf16[1024,128]{1,0:T(8,128)(2,1)} %win_hbm.1, ...), custom_call_target="tpu_custom_call" | custom-call | flops 4294967296 | bytes 4194304 | tf_op jit(solution)/shard_map/pallas_call | solution.py:594
  114.3 1.9 %copy.11 = bf16[256,1024]{1,0:T(8,128)(2,1)} copy(bf16[256,1024]{1,0:T(8,128)(2,1)} %shard_map.82) | data formatting | bytes 1048576

commit v6 on v5

--- a/solution.py
+++ b/solution.py
@@ -229,6 +229,22 @@
         slot = slot_of(1 - x, c, 1 - y, (z + k) % n_z)
         return [(None, slot, None, to_c, 5 + n_z * 8 + k)]
 
+    def sends_y_halves(k):
+        whole, relayed = sends_y(k)
+        return [(x == 0,) + whole[1:], (x == 1, whole[1], 0) + whole[3:], relayed]
+
+    def sends_x_halves(k):
+        slot = slot_of(1 - x, c, y, (z + k) % n_z)
+        return sends_x(k) + [(x == 0, slot, 1, to_y, 5 + n_z * 21 + k)]
+
+    def sends_corner_halves(k):
+        slot, base = slot_of(1 - x, c, 1 - y, (z + k) % n_z), 5 + n_z * 8 + k
+        return [
+            (x == 1, slot, None, to_c, base),
+            (x == 0, slot, 0, to_c, base),
+            (x == 0, slot, 1, to_c, 5 + n_z * 22 + k),
+        ]
+
     def sends_query(zz, part):
         slot = slot_of(0, 0, y, zz)
         base = 5 + n_z * 9 + zz * 10 + part * 5
@@ -273,11 +289,26 @@
         block = silu(jnp.dot(normed[...], w_all[slot], preferred_element_type=jnp.float32))
         proj[slot] = block.astype(jnp.bfloat16).reshape(tiles, tile_rows, width)
 
-    def relay(slot, listed, skip):
-        @pl.when(jnp.logical_not(skip))
-        def _():
-            arrived(w_copy, slot, None)
-            each(w_copy, listed, start)
+    def relay(slot, listed, skip, halves=None, w_listed=None):
+        w_listed = listed if w_listed is None else w_listed
+        if halves is None:
+
+            @pl.when(jnp.logical_not(skip))
+            def _():
+                arrived(w_copy, slot, None)
+                each(w_copy, w_listed, start)
+        else:
+
+            @pl.when(jnp.logical_not(skip) & halves)
+            def _():
+                for part in range(2):
+                    arrived(w_copy, slot, part)
+                    each(w_copy, [entry for entry in w_listed if entry[2] == part], start)
+
+            @pl.when(jnp.logical_not(skip | halves))
+            def _():
+                arrived(w_copy, slot, None)
+                each(w_copy, [entry for entry in w_listed if entry[2] is None], start)
 
         arrived(o_copy, slot, None)
         each(o_copy, listed, start)
@@ -465,8 +496,8 @@
 
     def side_step(k, carry):
         zz = (z + k) % n_z
-        relay(slot_of(x, c, 1 - y, zz), sends_y(k), is_query)
-        relay(slot_of(1 - x, c, y, zz), sends_x(k), x_is_query)
+        relay(slot_of(x, c, 1 - y, zz), sends_y(k), is_query, None, sends_y_halves(k))
+        relay(slot_of(1 - x, c, y, zz), sends_x(k), x_is_query, None, sends_x_halves(k))
         relay(slot_of(x, 1 - c, y, zz), [], sib_is_query)
         answer(n_z + k)
         return carry
@@ -475,7 +506,7 @@
 
     def corner_step(k, carry):
         zz = (z + k) % n_z
-        relay(slot_of(1 - x, c, 1 - y, zz), sends_corner(k), x_is_query)
+        relay(slot_of(1 - x, c, 1 - y, zz), sends_corner(k), x_is_query, x == 0, sends_corner_halves(k))
         relay(slot_of(x, 1 - c, 1 - y, zz), [], sib_is_query)
         relay(slot_of(1 - x, 1 - c, y, zz), [], diagonal_is_query)
         return carry
@@ -484,7 +515,7 @@
 
     def last_step(k, carry):
         slot = slot_of(1 - x, 1 - c, 1 - y, (z + k) % n_z)
-        relay(slot, [], diagonal_is_query)
+        relay(slot, [], diagonal_is_query, x == 0)
         return carry
 
     lax.fori_loop(0, n_z, last_step, 0)
@@ -551,8 +582,8 @@
         return carry
 
     def sent_rest(k, carry):
-        by_y, by_x = sends_y(k), sends_x(k) + sends_corner(k)
-        each(o_copy, by_y + by_x, sent)
+        by_y, by_x = sends_y_halves(k), sends_x_halves(k) + sends_corner_halves(k)
+        each(o_copy, sends_y(k) + sends_x(k) + sends_corner(k), sent)
 
         @pl.when(jnp.logical_not(is_query))
         def _():
@@ -584,7 +615,7 @@
     out_rows = weight_out.shape[0]
     tiles = tile_user.shape[0]
     tile_rows = row_total // tiles
-    sends = 5 + 21 * (n_usr // 2)
+    sends = 5 + 23 * (n_usr // 2)
     exchange = pltpu.VMEM((n_usr, HEADS, tile_rows, width), jnp.bfloat16)
     dma = pltpu.SemaphoreType.DMA
     in_any = pl.BlockSpec(memory_space=pl.ANY)

time: 117 us -> 109 us (0.932)
  Pallas kernels: 114 us -> 105 us
    pallas_call x1, Pallas kernels: 114 us -> 105 us  [fused_shards(): pl.pallas_call(functools.partial(layer_kernel, n_usr), out_shape=jax.Shap...]
where the time goes in v6:
time: 109 us; the launch traced here: 108 us
  Pallas kernels  105 us (96%)
  local copies, waits for them, and re-layouts  1.87 us (2%)
    pallas_call x1, Pallas kernels, fused_shards(): pl.pallas_call(functools.partial(layer_kernel, n_usr), out_shape=jax.Shap...  105 us

profile of v6, /device:TPU:1, one launch (start us, length us, event | category | flops | bytes accessed | tf_op | source)
XLA Modules:
  0.0 107.9 jit_solution(4092974496444386286)
XLA Ops:
  0.7 105.3 %shard_map.82 = bf16[256,1024]{1,0:T(8,128)(2,1)} custom-call(bf16[256,1024]{1,0:T(8,128)(2,1)} %cand_hbm.1, bf16[1,384,2048]{2,1,0:T(8,128)(2,1)} %kv_hbm.1, s32[1]{0:T(128)S(6)} %copy.10.len_ref, s32[1,3]{1,0:T(1,128)} %mask_ref.1, s32[1,4]{1,0:T(1,128)} %bitcast.1, s32[4]{0:T(128)} %count_ref.1, bf16[1024,128]{1,0:T(8,128)(2,1)} %win_hbm.1, ...), custom_call_target="tpu_custom_call" | custom-call | flops 4294967296 | bytes 4194304 | tf_op jit(solution)/shard_map/pallas_call | solution.py:625
  106.0 1.9 %copy.11 = bf16[256,1024]{1,0:T(8,128)(2,1)} copy(bf16[256,1024]{1,0:T(8,128)(2,1)} %shard_map.82) | data formatting | bytes 1048576

commit v7 on v6

--- a/solution.py
+++ b/solution.py
@@ -261,7 +261,7 @@
         slot = slot_of(0, 0, 1 - y, (z + k) % n_z)
         return [(None, slot, part, to_c, 5 + n_z * 19 + k * 2 + part)]
 
-    early, late = x == 1, (x == 0) & (c == 1)
+    early, late = jnp.logical_not(is_query), (x == 0) & (c == 1)
 
     def not_y(listed):
         return [entry for entry in listed if entry[3] is not to_y]
@@ -335,7 +335,7 @@
     loads[1].wait()
     pl.semaphore_wait(barrier, len(peers))
 
-    @pl.when(early)
+    @pl.when(x == 1)
     def _():
         each(w_copy, sends_across() + not_y(sends_own()), start)
 
@@ -353,6 +353,11 @@
                 each(w_copy, sends_query(zz, part), start)
 
     query_relay(z, is_query)
+
+    @pl.when(late)
+    def _():
+        each(w_copy, sends_across() + not_y(sends_own()), start)
+
     project(slot_of(0, 0, y, z))
 
     def query_line(k, carry):
@@ -456,10 +461,6 @@
         attend(source_of(k), answers)
         answer_copy(k).start()
 
-    @pl.when(late)
-    def _():
-        each(w_copy, sends_own() + sends_across(), start)
-
     @pl.when(early)
     def _():
         each(w_copy, only_y(sends_own()), start)
@@ -483,13 +484,14 @@
     attend(u, returned)
 
     def line_step(k, carry):
+        answer(k)
         for zz in (z - k, z + k):
 
             @pl.when((zz >= 0) & (zz < n_z))
             def _(zz=zz):
-                relay(slot_of(x, c, y, zz), sends_line(zz), jnp.logical_not(late))
-
-        answer(k)
+                arrived(o_copy, slot_of(x, c, y, zz), None)
+                each(o_copy, sends_line(zz), start)
+
         return carry
 
     lax.fori_loop(1, n_z, line_step, 0)

time: 109 us -> 118 us (1.083)
  Pallas kernels: 105 us -> 113 us
    pallas_call x1, Pallas kernels: 105 us -> 113 us  [fused_shards(): pl.pallas_call(functools.partial(layer_kernel, n_usr), out_shape=jax.Shap...]
where the time goes in v7:
time: 118 us; the launch traced here: 116 us
  Pallas kernels  113 us (96%)
  local copies, waits for them, and re-layouts  1.87 us (2%)
    pallas_call x1, Pallas kernels, fused_shards(): pl.pallas_call(functools.partial(layer_kernel, n_usr), out_shape=jax.Shap...  113 us

profile of v7, /device:TPU:1, one launch (start us, length us, event | category | flops | bytes accessed | tf_op | source)
XLA Modules:
  0.0 115.8 jit_solution(8826729038419970539)
XLA Ops:
  0.7 113.3 %shard_map.82 = bf16[256,1024]{1,0:T(8,128)(2,1)} custom-call(bf16[256,1024]{1,0:T(8,128)(2,1)} %cand_hbm.1, bf16[1,384,2048]{2,1,0:T(8,128)(2,1)} %kv_hbm.1, s32[1]{0:T(128)S(6)} %copy.10.len_ref, s32[1,3]{1,0:T(1,128)} %mask_ref.1, s32[1,4]{1,0:T(1,128)} %bitcast.1, s32[4]{0:T(128)} %count_ref.1, bf16[1024,128]{1,0:T(8,128)(2,1)} %win_hbm.1, ...), custom_call_target="tpu_custom_call" | custom-call | flops 4294967296 | bytes 4194304 | tf_op jit(solution)/shard_map/pallas_call | solution.py:627
  113.9 1.9 %copy.11 = bf16[256,1024]{1,0:T(8,128)(2,1)} copy(bf16[256,1024]{1,0:T(8,128)(2,1)} %shard_map.82) | data formatting | bytes 1048576

commit v8 on v6

--- a/solution.py
+++ b/solution.py
@@ -483,13 +483,13 @@
     attend(u, returned)
 
     def line_step(k, carry):
+        answer(k)
         for zz in (z - k, z + k):
 
             @pl.when((zz >= 0) & (zz < n_z))
             def _(zz=zz):
                 relay(slot_of(x, c, y, zz), sends_line(zz), jnp.logical_not(late))
 
-        answer(k)
         return carry
 
     lax.fori_loop(1, n_z, line_step, 0)

time: 109 us -> 112 us (1.028)
  Pallas kernels: 105 us -> 108 us
    pallas_call x1, Pallas kernels: 105 us -> 108 us  [fused_shards(): pl.pallas_call(functools.partial(layer_kernel, n_usr), out_shape=jax.Shap...]
where the time goes in v8:
time: 112 us; the launch traced here: 111 us
  Pallas kernels  108 us (96%)
  local copies, waits for them, and re-layouts  1.87 us (2%)
    pallas_call x1, Pallas kernels, fused_shards(): pl.pallas_call(functools.partial(layer_kernel, n_usr), out_shape=jax.Shap...  108 us

profile of v8, /device:TPU:1, one launch (start us, length us, event | category | flops | bytes accessed | tf_op | source)
XLA Modules:
  0.0 110.7 jit_solution(8219330374988512070)
XLA Ops:
  0.7 108.2 %shard_map.82 = bf16[256,1024]{1,0:T(8,128)(2,1)} custom-call(bf16[256,1024]{1,0:T(8,128)(2,1)} %cand_hbm.1, bf16[1,384,2048]{2,1,0:T(8,128)(2,1)} %kv_hbm.1, s32[1]{0:T(128)S(6)} %copy.10.len_ref, s32[1,3]{1,0:T(1,128)} %mask_ref.1, s32[1,4]{1,0:T(1,128)} %bitcast.1, s32[4]{0:T(128)} %count_ref.1, bf16[1024,128]{1,0:T(8,128)(2,1)} %win_hbm.1, ...), custom_call_target="tpu_custom_call" | custom-call | flops 4294967296 | bytes 4194304 | tf_op jit(solution)/shard_map/pallas_call | solution.py:625
  108.8 1.9 %copy.11 = bf16[256,1024]{1,0:T(8,128)(2,1)} copy(bf16[256,1024]{1,0:T(8,128)(2,1)} %shard_map.82) | data formatting | bytes 1048576
